TPU v7x, 32 devices: a whole 2x2x4 slice. The times are simulated.
32 devices in a mesh: groups: 2 (over x), pool: 8 (over z, y), head: 2 (over core).
Axes of the slice: x: 2, y: 2, z: 4, core: 2. Of those that a mesh axis runs over, the one named last changes fastest.
Arguments:
- tokens: bfloat16 [128, 7168], P(('groups', 'pool')), parts along dimension 0, may hold values from -6 to 6
- queries: bfloat16 [128, 64, 576], P(('groups', 'pool'), 'head'), parts along dimension 0, may hold values from -60 to 60
- cache_latent: bfloat16 [128, 512, 576], P(('groups', 'pool')), parts along dimension 0, may hold values from -6 to 6
- page_lists: int32 [128, 4], P(('groups', 'pool')), parts along dimension 0, may hold values from 0 to 7, as said below
- cache_lengths: int32 [128], P(('groups', 'pool')), parts along dimension 0, may hold values from 256 to 512, as said below
- value_up: bfloat16 [2, 32, 512, 128], P('head', 'pool'), may hold values from -0.25 to 0.25
- out_proj: bfloat16 [2, 32, 128, 7168], P('head', 'pool'), may hold values from -0.25 to 0.25
- norm_gain: float32 [7168], replicated, may hold values from 0.1 to 1.9
- expert_ids: int32 [128, 2], P(('groups', 'pool')), parts along dimension 0, may hold values from 0 to 3, all different within a row; in each aligned block of 8 rows (0 to 7, 8 to 15, ...) at most 8 rows name the same one
- route_weights: float32 [128, 2], P(('groups', 'pool')), parts along dimension 0, may hold values from 0.2 to 2
- gate_proj: bfloat16 [8, 7168, 1024], P('pool', None, 'head'), may hold values from -0.0625 to 0.0625
- up_proj: bfloat16 [8, 7168, 1024], P('pool', None, 'head'), may hold values from -0.0625 to 0.0625
- down_proj: bfloat16 [8, 1024, 7168], P('pool', 'head'), may hold values from -0.125 to 0.125
Outputs:
- mixed: bfloat16 [128, 7168], P(('groups', 'pool')), parts along dimension 0
There are 2 independent parts, one for each index of `groups`. A program takes and returns all parts, laid end to end along the dimension named above; an argument that names none is the same for every part. Nothing has to cross between parts.
Inputs may be any that keep to these rules, and one draw needn't show every extreme that they name: `page_lists`: each row names 4 different pages of its stream, page 0 and the page that holds the stream's last cached position among them, and only pages that begin below the stream's cache length. `cache_lengths`: some stream of every part has all 512 positions cached. `expert_ids`: each row names 2 different experts.
All inputs are finite; a program needn't handle non-finite values.
Results may differ from a plain program's by a relative error of at most 0.018.
Values may be sent and summed in bfloat16 or wider, within the bound.
A program may use at most 128 MiB of HBM per device.

v0:
```python
import jax
import jax.numpy as jnp
from jax import lax
from jax.sharding import PartitionSpec as P

D = 7168
LATENT = 512
EXPERTS = 4
PAGE = 64
KDIM = 576
NPAGE = 8
KEYS = 256


softmax_scale = 192 ** (-0.5)


def attend(queries, cache_latent, page_lists, cache_lengths):
    streams = queries.shape[0]
    pages = cache_latent.reshape(streams, NPAGE, PAGE, KDIM)
    picked = jnp.take_along_axis(pages, page_lists[:, :, None, None], axis=1).reshape(
        streams, KEYS, KDIM
    )
    offsets = (
        page_lists[:, :, None] * PAGE + jnp.arange(PAGE, dtype=jnp.int32)[None, None, :]
    ).reshape(streams, KEYS)
    usable = offsets < cache_lengths[:, None]
    scores = (
        jnp.einsum("shc,skc->shk", queries, picked, preferred_element_type=jnp.float32)
        * softmax_scale
    )
    scores = jnp.where(usable[:, None, :], scores, -1e30)
    top = jnp.max(scores, axis=-1, keepdims=True)
    weighed = jnp.exp(scores - top) * usable[:, None, :].astype(jnp.float32)
    probs = (weighed / jnp.sum(weighed, axis=-1, keepdims=True)).astype(jnp.bfloat16)
    return jnp.einsum(
        "shk,skc->shc", probs, picked[:, :, :LATENT], preferred_element_type=jnp.float32
    ).astype(jnp.bfloat16)


def route_slots(expert_ids):
    streams, routes_each = expert_ids.shape
    flat_ids = expert_ids.reshape(streams * routes_each)
    onehot = (flat_ids[:, None] == jnp.arange(EXPERTS, dtype=jnp.int32)[None, :]).astype(jnp.int32)
    earlier = jnp.cumsum(onehot, axis=0) - onehot
    return jnp.sum(earlier * onehot, axis=1).reshape(streams, routes_each)


def per_device(
    tokens,
    queries,
    cache_latent,
    page_lists,
    cache_lengths,
    value_up,
    out_proj,
    norm_gain,
    expert_ids,
    route_weights,
    gate_proj,
    up_proj,
    down_proj,
):
    local_streams = tokens.shape[0]
    pool_size = lax.axis_size("pool")
    latent_out = attend(queries, cache_latent, page_lists, cache_lengths)
    by_head = lax.all_to_all(latent_out, "pool", split_axis=1, concat_axis=0, tiled=True)
    head_values = jnp.einsum(
        "shc,hcv->shv", by_head, value_up[0], preferred_element_type=jnp.float32
    ).astype(jnp.bfloat16)
    attn_part = lax.psum_scatter(
        jnp.einsum(
            "shv,hvd->sd", head_values, out_proj[0], preferred_element_type=jnp.float32
        ).astype(jnp.bfloat16),
        "pool",
        scatter_dimension=0,
        tiled=True,
    )
    attn_out = lax.psum(attn_part, "head").astype(jnp.float32)
    residual = tokens.astype(jnp.float32) + attn_out
    scale_back = lax.rsqrt(jnp.mean(residual * residual, axis=-1, keepdims=True) + 1e-06)
    normed = (residual * scale_back * norm_gain[None, :]).astype(jnp.bfloat16)
    slots = route_slots(expert_ids)
    match_expert = (
        expert_ids[None, None, :, :] == jnp.arange(EXPERTS, dtype=jnp.int32)[:, None, None, None]
    )
    match_slot = (
        slots[None, None, :, :] == jnp.arange(local_streams, dtype=jnp.int32)[None, :, None, None]
    )
    matched = match_expert & match_slot
    placing = jnp.sum(matched.astype(jnp.float32), axis=-1).astype(jnp.bfloat16)
    combining = jnp.sum(jnp.where(matched, route_weights[None, None, :, :], 0.0), axis=-1)
    outgoing = jnp.einsum(
        "ect,td->ecd", placing, normed, preferred_element_type=jnp.float32
    ).astype(jnp.bfloat16)
    span_size = pool_size // EXPERTS
    outgoing = jnp.broadcast_to(outgoing[:, None], (EXPERTS, span_size, local_streams, D)).reshape(
        pool_size, local_streams, D
    )
    received = lax.all_to_all(outgoing, "pool", split_axis=0, concat_axis=0, tiled=True)
    expert_rows = received.reshape(pool_size * local_streams, D)
    gate_val = jnp.dot(expert_rows, gate_proj[0], preferred_element_type=jnp.float32)
    up_val = jnp.dot(expert_rows, up_proj[0], preferred_element_type=jnp.float32)
    activated = (jax.nn.silu(gate_val) * up_val).astype(jnp.bfloat16)
    partial_out = jnp.dot(activated, down_proj[0], preferred_element_type=jnp.float32).astype(
        jnp.bfloat16
    )
    partial_out = partial_out.reshape(pool_size, local_streams, D)
    returned = lax.all_to_all(partial_out, "pool", split_axis=0, concat_axis=0, tiled=True)
    expert_out = jnp.sum(
        returned.reshape(EXPERTS, span_size, local_streams, D).astype(jnp.float32), axis=1
    )
    moe_part = jnp.einsum("ect,ecd->td", combining, expert_out, precision=lax.Precision.HIGHEST)
    moe_out = lax.psum(moe_part.astype(jnp.bfloat16), "head").astype(jnp.float32)
    return (residual + moe_out).astype(jnp.bfloat16)


def solution(mesh):
    return jax.shard_map(
        per_device,
        mesh=mesh,
        in_specs=(
            P(("groups", "pool"), None),
            P(("groups", "pool"), "head", None),
            P(("groups", "pool"), None, None),
            P(("groups", "pool"), None),
            P(("groups", "pool")),
            P("head", "pool", None, None),
            P("head", "pool", None, None),
            P(),
            P(("groups", "pool"), None),
            P(("groups", "pool"), None),
            P("pool", None, "head"),
            P("pool", None, "head"),
            P("pool", "head", None),
        ),
        out_specs=P(("groups", "pool"), None),
        check_vma=False,
    )
```

profile of v0, /device:TPU:0, one launch (start us, length us, event | category | flops | bytes accessed | tf_op | source)
XLA Modules:
  0.0 227.6 jit_solution(11745490610033422616)
XLA Ops:
  6.5 0.7 bitcast_or_fusion
  7.3 0.7 compare_and_fusion
  8.0 0.7 broadcast_multiply_fusion
  8.7 7.7 %copy.51 = bf16[8,512,576]{2,1,0:T(8,128)(2,1)} copy(bf16[8,512,576]{1,2,0:T(8,128)(2,1)} %param.15) | data formatting | bytes 9437184 | tf_op args[2]
  16.4 0.1 reshape.136
  16.5 0.1 copy.50
  16.7 0.1 broadcast_in_dim.59
  16.9 0.1 add.61
  17.0 0.1 add.63
  17.1 4.9 %gather_fusion = bf16[32,64,576]{2,1,0:T(8,128)(2,1)} fusion(bf16[8,8,64,576]{3,2,1,0:T(8,128)(2,1)} %bitcast.74, s32[32]{0:T(128)S(1)} %reshape.136), kind=kCustom, calls=%fused_computation | custom fusion | bytes 4718848 | tf_op jit(solution)/shard_map/jit(take_along_axis)/gather | solution.py:21
  22.0 2.0 bitcast_select_fusion
  24.1 0.9 fusion.19
  25.0 0.7 copy-done.4
  25.7 0.2 fusion.57
  25.9 1.5 fusion.13
  27.4 0.2 copy.54
  27.6 16.0 %all_to_all.28 = bf16[8,32,512]{2,0,1:T(8,128)(2,1)S(1)} all-to-all(bf16[8,32,512]{2,0,1:T(8,128)(2,1)S(1)} %copy.54), channel_id=1, replica_groups=mesh['groups'=2,'pool'=8,'head'=2] {'pool'}, dimensions={1} | all-to-all | bytes 524288 | tf_op jit(solution)/shard_map/all_to_all | solution.py:67
  43.6 5.6 %fusion.1 = bf16[64,7168]{1,0:T(8,128)(2,1)} fusion(bf16[1,4,128,7168]{3,2,1,0:T(8,128)(2,1)} %param.19, bf16[1,4,512,128]{3,2,1,0:T(8,128)(2,1)S(1)} %copy-done, bf16[8,8,4,512]{3,1,2,0:T(8,128)(2,1)S(1)} %bitcast.77), kind=kOutput, calls=%fused_computation.4 | convolution fusion | flops 503808000 | bytes 9043968 | tf_op jit(solution)/shard_map/shv,hvd->sd/dot_general | solution.py:72
  49.6 0.2 select_reduce_fusion
  49.9 0.1 copy.57
  50.0 61.8 %reduce-scatter.2.cloned.1.call-done = bf16[8,7168]{1,0:T(8,128)(2,1)} async-done(((bf16[64,7168]{1,0:T(8,128)(2,1)}), bf16[8,7168]{1,0:T(8,128)(2,1)}) %reduce-scatter.2.cloned.1.call-update) | async-done | bytes 114704 | tf_op jit(solution)/shard_map/reduce_scatter | solution.py:71
  111.9 19.2 %all-reduce.3.cloned.1.call-done = bf16[8,7168]{1,0:T(8,128)(2,1)} async-done(((bf16[8,7168]{1,0:T(8,128)(2,1)}), bf16[8,7168]{1,0:T(8,128)(2,1)}) %all-reduce.3.cloned.1.call-update) | async-done | bytes 114704 | tf_op jit(solution)/shard_map/psum | solution.py:79
  131.1 1.1 multiply_reduce_fusion
  132.2 1.2 convolution_convert_fusion.1
  133.5 29.3 %all_to_all.29 = bf16[8,8,7168]{2,1,0:T(8,128)(2,1)S(1)} all-to-all(bf16[8,8,7168]{2,1,0:T(8,128)(2,1)S(1)} %bitcast.76), channel_id=1, replica_groups=mesh['groups'=2,'pool'=8,'head'=2] {'pool'}, dimensions={0} | all-to-all | bytes 1835008 | tf_op jit(solution)/shard_map/all_to_all | solution.py:100
  162.8 4.5 %fusion.7 = f32[64,512]{1,0:T(8,128)S(1)} fusion(bf16[1,7168,512]{2,1,0:T(8,128)(2,1)} %param.23, bf16[8,8,7168]{2,1,0:T(8,128)(2,1)S(1)} %all_to_all.29), kind=kOutput, calls=%fused_computation.12 | convolution fusion | flops 469762048 | bytes 8388608 | tf_op jit(solution)/shard_map/dot_general | solution.py:102
  167.2 7.9 %fusion.2 = bf16[8,8,7168]{2,1,0:T(8,128)(2,1)S(1)} fusion(bf16[1,512,7168]{2,1,0:T(8,128)(2,1)} %param.25, bf16[1,7168,512]{2,1,0:T(8,128)(2,1)} %param.24, bf16[8,8,7168]{2,1,0:T(8,128)(2,1)S(1)} %all_to_all.29, f32[64,512]{1,0:T(8,128)S(1)} %fusion.7), kind=kOutput, calls=%fused_computation.5 | convolution fusion | flops 940179456 | bytes 16646144 | tf_op jit(solution)/shard_map/dot_general | solution.py:105
  175.2 26.3 %all_to_all.30 = bf16[8,8,7168]{2,1,0:T(8,128)(2,1)S(1)} all-to-all(bf16[8,8,7168]{2,1,0:T(8,128)(2,1)S(1)} %fusion.2), channel_id=1, replica_groups=mesh['groups'=2,'pool'=8,'head'=2] {'pool'}, dimensions={0} | all-to-all | bytes 1835008 | tf_op jit(solution)/shard_map/all_to_all | solution.py:109
  201.5 0.1 convert_reduce_fusion
  201.6 1.2 fusion.3
  202.9 16.7 %all-reduce.5.cloned.1.call-done = bf16[8,7168]{1,0:T(8,128)(2,1)} async-done(((bf16[8,7168]{1,0:T(8,128)(2,1)}), bf16[8,7168]{1,0:T(8,128)(2,1)}) %all-reduce.5.cloned.1.call-update) | async-done | bytes 114704 | tf_op jit(solution)/shard_map/psum | solution.py:114
  219.5 1.6 add_convert_fusion
  (39 shorter events, 1.0 us)
Async XLA Ops:
  6.5 37.1 %copy-start = (bf16[1,4,512,128]{3,2,1,0:T(8,128)(2,1)S(1)}, bf16[1,4,512,128]{3,2,1,0:T(8,128)(2,1)}, u32[]{:S(2)}) copy-start(bf16[1,4,512,128]{3,2,1,0:T(8,128)(2,1)} %param.18) | copy-start | bytes 1572868
  6.5 105.3 %reduce-scatter.2.cloned.1.call-start = ((), (), s32[]{:S(2)}) async-start(), calls=%async_computation.4 | async-start | bytes 1032192 | tf_op jit(solution)/shard_map/reduce_scatter | solution.py:71
  17.1 6.9 %copy-start.8 = (s32[8]{0:T(128)S(1)}, s32[8]{0:T(128)}, u32[]{:S(2)}) copy-start(s32[8]{0:T(128)} %param.17) | copy-start | bytes 100
  17.1 7.0 %copy-start.3 = (bf16[8,32,576]{2,1,0:T(8,128)(2,1)S(1)}, bf16[8,32,576]{2,1,0:T(8,128)(2,1)}, u32[]{:S(2)}) copy-start(bf16[8,32,576]{2,1,0:T(8,128)(2,1)} %param.14) | copy-start | bytes 884740
  25.0 0.7 copy-start.4
  43.6 5.7 %copy-start.6 = (s32[8,2]{0,1:T(2,128)S(1)}, s32[8,2]{0,1:T(2,128)}, u32[]{:S(2)}) copy-start(s32[8,2]{0,1:T(2,128)} %param.21) | copy-start | bytes 196
  43.6 68.3 %copy-start.7 = (f32[8,2]{0,1:T(2,128)S(1)}, f32[8,2]{0,1:T(2,128)}, u32[]{:S(2)}) copy-start(f32[8,2]{0,1:T(2,128)} %param.22) | copy-start | bytes 196
  43.6 87.5 %copy-start.1 = (bf16[8,7168]{1,0:T(8,128)(2,1)S(1)}, bf16[8,7168]{1,0:T(8,128)(2,1)}, u32[]{:S(2)}) copy-start(bf16[8,7168]{1,0:T(8,128)(2,1)} %param.13) | copy-start | bytes 344068
  43.6 88.5 %copy-start.5 = (f32[7168]{0:T(1024)S(1)}, f32[7168]{0:T(1024)}, u32[]{:S(2)}) copy-start(f32[7168]{0:T(1024)} %param.20) | copy-start | bytes 86020
  49.3 81.8 %all-reduce.3.cloned.1.call-start = ((), (), s32[]{:S(2)}) async-start(), calls=%async_computation.5 | async-start | bytes 229376 | tf_op jit(solution)/shard_map/psum | solution.py:79
  111.8 107.7 %all-reduce.5.cloned.1.call-start = ((), (), s32[]{:S(2)}) async-start(), calls=%async_computation.6 | async-start | bytes 229376 | tf_op jit(solution)/shard_map/psum | solution.py:114
  175.1 44.4 %copy-start.2 = (bf16[8,7168]{1,0:T(8,128)(2,1)S(1)}, bf16[8,7168]{1,0:T(8,128)(2,1)}, u32[]{:S(2)}) copy-start(bf16[8,7168]{1,0:T(8,128)(2,1)} %all-reduce.3.cloned.1.call-done) | copy-start | bytes 344068
Sparse Core Ops, SparseCore 0:
  49.4 62.3 reduce-scatter.1
  114.2 16.8 all-reduce.2
  203.0 16.4 all-reduce.4
where the time goes:
time: 228 us
  waiting for transfers between devices  97.7 us (43%)
  blocking collectives  71.7 us (31%)
  matrix products  22.8 us (10%)
  local copies, waits for them, and re-layouts  14.6 us (6%)
  between operations  13.3 us (6%)
  other arithmetic  7.48 us (3%)
    reduce_scatter x1, waiting for transfers between devices, per_device(): lax.psum_scatter(jnp.einsum('shv,hvd->sd', head_values, out_proj[0], pref...  61.8 us
    all_to_all x1, blocking collectives, per_device(): lax.all_to_all(outgoing, 'pool', split_axis=0, concat_axis=0, tiled=True)  29.3 us
    all_to_all x1, blocking collectives, per_device(): lax.all_to_all(partial_out, 'pool', split_axis=0, concat_axis=0, tiled=True)  26.3 us
    psum x1, waiting for transfers between devices, per_device(): attn_out = lax.psum(attn_part, 'head').astype(jnp.float32)  19.2 us
    psum x1, waiting for transfers between devices, per_device(): lax.psum(moe_part.astype(jnp.bfloat16), 'head').astype(jnp.float32)  16.7 us
    all_to_all x1, blocking collectives, per_device(): lax.all_to_all(latent_out, 'pool', split_axis=1, concat_axis=0, tiled=True)  16 us
    unnamed x20, local copies, waits for them, and re-layouts  8.49 us
    dot_general x1, matrix products, per_device(): jnp.dot(activated, down_proj[0], preferred_element_type=jnp.float32)  7.91 us
  transfers between devices with their start and end apart: 3, of which 3 were waited for; matrix products, arithmetic and copies ran while one was open for 0% of the time, Pallas kernels for 0%

commit v1 on v0

v1 whole, which is shorter than its diff:
```python
import functools

import jax
import jax.numpy as jnp
from jax import lax
from jax.experimental import pallas as pl
from jax.experimental.pallas import tpu as pltpu
from jax.sharding import PartitionSpec as P

LATENT = 512
EXPERTS = 4
PAGE = 64
CHUNKS = 2
SCALE = 192 ** (-0.5)
MESH = pl.DeviceIdType.MESH
BF16 = jnp.bfloat16
F32 = jnp.float32


def log2(n):
    assert n & (n - 1) == 0
    return n.bit_length() - 1


def dot(a, b):
    return jnp.dot(a, b, preferred_element_type=F32)


def kernel(
    pool,
    tok_hbm, q_hbm, cache_hbm, pages_ref, lens_ref, vu_hbm, op_hbm, gain_ref, ids_ref, rw_ref,
    g_hbm, u_hbm, d_hbm,
    out_ref,
    tok, q, cache, vu, op, gw, uw, dw,
    scores, lat, a_buf, a_recv, x_buf, x_recv, r_buf, r_recv, c_recv, resid, o_buf,
    k_sem, w_sem, a_s, a_r, x_s, x_r, r_s, r_r, c_s, c_r, f_s, f_r, o_s, o_r,
):
    p = lax.axis_index("pool")
    h = lax.axis_index("head")
    oh = 1 - h
    ns, nh, _ = q.shape
    ctx = cache.shape[1]
    hh_n = vu.shape[0]
    width = tok.shape[1]
    half = width // 2
    ck = half // CHUNKS
    cq = ck // 2
    rows = ns * nh
    toks = pool * ns
    block_w = CHUNKS * cq

    load_q = pltpu.make_async_copy(q_hbm, q, w_sem.at[0])
    load_q.start()
    load_k = [pltpu.make_async_copy(cache_hbm.at[s], cache.at[s], k_sem.at[s]) for s in range(ns)]
    for copy in load_k:
        copy.start()
    load_vu = pltpu.make_async_copy(vu_hbm, vu, w_sem.at[1])
    load_op = pltpu.make_async_copy(op_hbm, op, w_sem.at[2])
    load_tok = pltpu.make_async_copy(tok_hbm, tok, w_sem.at[3])
    load_g = pltpu.make_async_copy(g_hbm, gw, w_sem.at[4])
    load_u = pltpu.make_async_copy(u_hbm, uw, w_sem.at[5])
    load_d = pltpu.make_async_copy(d_hbm, dw, w_sem.at[6])
    for copy in (load_vu, load_op, load_tok, load_g, load_u, load_d):
        copy.start()

    def peer(d):
        return lax.rem(p + d, pool)

    def source(d):
        return lax.rem(p + pool - d, pool)

    barrier = pltpu.get_barrier_semaphore()

    def greet(d, carry):
        pl.semaphore_signal(barrier, inc=1, device_id={"pool": peer(d)}, device_id_type=MESH)
        return carry

    lax.fori_loop(1, pool, greet, 0)
    pl.semaphore_signal(barrier, inc=1, device_id={"head": oh}, device_id_type=MESH)

    def to_pool(src, dst, send, recv, to):
        return pltpu.make_async_remote_copy(
            src_ref=src, dst_ref=dst, send_sem=send, recv_sem=recv,
            device_id={"pool": to}, device_id_type=MESH,
        )

    def to_core(src, dst, send, recv):
        return pltpu.make_async_remote_copy(
            src_ref=src, dst_ref=dst, send_sem=send, recv_sem=recv,
            device_id={"head": oh}, device_id_type=MESH,
        )

    def each(body):
        def step(d, carry):
            body(d)
            return carry

        lax.fori_loop(1, pool, step, 0)

    pos = lax.broadcasted_iota(jnp.int32, (ns, ctx), 1)
    page = pos >> log2(PAGE)
    listed = pages_ref[:, 0:1] == page
    for j in range(1, pages_ref.shape[1]):
        listed = listed | (pages_ref[:, j : j + 1] == page)
    usable = jnp.where(listed & (pos < lens_ref[:, 0:1]), 1.0, 0.0)
    load_q.wait()
    for s in range(ns):
        load_k[s].wait()
        scores[s] = lax.dot_general(
            q[s], cache[s], (((1,), (1,)), ((), ())), preferred_element_type=F32
        )
    for s in range(ns):
        keep = usable[s : s + 1, :] > 0.5
        sc = jnp.where(keep, scores[s] * SCALE, -1e30)
        top = jnp.max(sc, axis=-1, keepdims=True)
        weighed = jnp.where(keep, jnp.exp(sc - top), 0.0)
        probs = (weighed / jnp.sum(weighed, axis=-1, keepdims=True)).astype(BF16)
        lat[s * nh : (s + 1) * nh, :] = dot(probs, cache[s, :, :LATENT]).astype(BF16)

    per = ns * hh_n
    ri = lax.broadcasted_iota(jnp.int32, (rows, 1), 0)
    rest = ri & (per - 1)
    origin = (rest >> log2(hh_n)) * nh + (ri >> log2(per)) * hh_n + (rest & (hh_n - 1))
    ci = lax.broadcasted_iota(jnp.int32, (rows, rows), 1)
    perm = jnp.where(ci == origin, 1.0, 0.0).astype(BF16)
    a_buf[...] = dot(perm, lat[...]).reshape(pool, per, LATENT).astype(BF16)
    pl.semaphore_wait(barrier, pool)

    def a_copy(d, slot):
        return to_pool(a_buf.at[peer(d)], a_recv.at[slot], a_s.at[d], a_r.at[d], peer(d))

    each(lambda d: a_copy(d, p).start())
    a_recv[p] = a_buf[p]
    load_vu.wait()
    each(lambda d: a_copy(d, source(d)).wait_recv())
    got = a_recv[...].astype(F32).reshape(rows, LATENT).astype(BF16)
    values = []
    ti = lax.broadcasted_iota(jnp.int32, (toks, rows), 0)
    tj = lax.broadcasted_iota(jnp.int32, (toks, rows), 1)
    for hh in range(hh_n):
        if hh_n > 1:
            pick = jnp.where(tj == ti * hh_n + hh, 1.0, 0.0).astype(BF16)
            mine = dot(pick, got).astype(BF16)
        else:
            mine = got
        values.append(dot(mine, vu[hh]).astype(BF16))
    head_values = jnp.concatenate(values, axis=1) if hh_n > 1 else values[0]

    def x_copy(i, c):
        return to_core(x_buf.at[i, c], x_recv.at[i, c], x_s.at[i, c], x_r.at[i, c])

    def r_copy(i, c, d, slot):
        return to_pool(
            r_buf.at[i, c, peer(d)], r_recv.at[i, c, slot], r_s.at[i, c, d], r_r.at[i, c, d], peer(d)
        )

    def columns(side, c, j=0, size=ck):
        return pl.ds(pl.multiple_of(side * half + (c * ck + j * cq), 128), size)

    def reduce_send(i, lhs, weights, by):
        for c in range(CHUNKS):
            v = dot(lhs, weights[:, columns(oh, c)])
            if by is not None:
                v = v * by
            x_buf[i, c] = v.astype(BF16)
            x_copy(i, c).start()
        for c in range(CHUNKS):
            v = dot(lhs, weights[:, columns(h, c)])
            if by is not None:
                v = v * by
            x_copy(i, c).wait_recv()
            v = v + x_recv[i, c].astype(F32)
            low = v[:, :cq].reshape(pool, ns, cq)
            high = v[:, cq:].reshape(pool, ns, cq)
            r_buf[i, c] = jnp.concatenate([low, high], axis=1).astype(BF16)
            each(lambda d: r_copy(i, c, d, p).start())
            r_recv[i, c, p] = r_buf[i, c, p]

    def reduced(i, c):
        each(lambda d: r_copy(i, c, d, source(d)).wait_recv())
        return jnp.sum(r_recv[i, c].astype(F32), axis=0)

    load_op.wait()
    reduce_send(0, head_values, op, None)

    load_tok.wait()
    squares = jnp.zeros((ns, 1), F32)
    for c in range(CHUNKS):
        total = reduced(0, c)
        tokens = jnp.concatenate(
            [tok[:, columns(h, c, j, cq)].astype(F32) for j in range(2)], axis=0
        )
        gain = jnp.concatenate(
            [jnp.broadcast_to(gain_ref[0:1, columns(h, c, j, cq)], (ns, cq)) for j in range(2)], axis=0
        )
        res = tokens + total
        resid[c] = res
        both = jnp.sum(res * res, axis=-1, keepdims=True)
        squares = squares + both[:ns] + both[ns:]
        c_recv[h, p, :, c * cq : (c + 1) * cq] = (res * gain).astype(BF16)
    lane = lax.broadcasted_iota(jnp.int32, (ns, 128), 1)
    extra = jnp.broadcast_to(squares, (ns, 128))
    extra = jnp.where(lane < EXPERTS, 0.0, extra)
    for k in range(ids_ref.shape[1]):
        extra = extra + jnp.where(lane == ids_ref[:, k : k + 1], rw_ref[:, k : k + 1], 0.0)
    upper = extra.astype(BF16).astype(F32)
    c_recv[h, p, :, block_w:] = jnp.concatenate([upper, extra - upper], axis=0).astype(BF16)

    def c_copy(d, slot):
        return to_pool(c_recv.at[h, slot], c_recv.at[h, slot], c_s.at[d], c_r.at[d], peer(d))

    def f_copy(d, side, slot):
        return to_core(c_recv.at[side, slot], c_recv.at[side, slot], f_s.at[d], f_r.at[d])

    each(lambda d: c_copy(d, p).start())
    f_copy(0, h, p).start()
    load_g.wait()
    load_u.wait()

    def pass_on(d):
        c_copy(d, source(d)).wait_recv()
        f_copy(d, h, source(d)).start()

    each(pass_on)

    def project(side):
        gate = up = None
        for c in range(CHUNKS):
            part = c_recv[side, :, :, c * cq : (c + 1) * cq].astype(F32)
            x = jnp.concatenate(
                [part[:, j * ns : (j + 1) * ns].reshape(toks, cq) for j in range(2)], axis=1
            ).astype(BF16)
            g = dot(x, gw[columns(side, c), :])
            u = dot(x, uw[columns(side, c), :])
            gate = g if gate is None else gate + g
            up = u if up is None else up + u
        part = c_recv[side, :, :, block_w:].astype(F32)
        return gate, up, (part[:, :ns] + part[:, ns:]).reshape(toks, 128)

    gate0, up0, extra0 = project(h)
    f_copy(0, oh, p).wait_recv()
    each(lambda d: f_copy(d, oh, source(d)).wait_recv())
    gate1, up1, extra1 = project(oh)
    lane = lax.broadcasted_iota(jnp.int32, (toks, 128), 1)
    expert = p // (pool // EXPERTS)
    share = jnp.sum(jnp.where(lane == expert, extra0, 0.0), axis=-1, keepdims=True)
    squares = jnp.sum(jnp.where(lane == EXPERTS, extra0 + extra1, 0.0), axis=-1, keepdims=True)
    back = lax.rsqrt(squares / width + 1e-06)
    gate = (gate0 + gate1) * back
    up = (up0 + up1) * back
    act = (gate / (1.0 + jnp.exp(-gate)) * up).astype(BF16)

    load_d.wait()
    reduce_send(1, act, dw, share)
    for c in range(CHUNKS):
        o_buf[h, c] = (resid[c] + reduced(1, c)).astype(BF16)

    def o_copy(side):
        return to_core(o_buf.at[side], o_buf.at[side], o_s.at[0], o_r.at[0])

    o_copy(h).start()

    def sent(d):
        a_copy(d, p).wait_send()
        c_copy(d, p).wait_send()
        f_copy(d, h, source(d)).wait_send()
        for i in range(2):
            for c in range(CHUNKS):
                r_copy(i, c, d, p).wait_send()

    each(sent)
    f_copy(0, h, p).wait_send()
    for i in range(2):
        for c in range(CHUNKS):
            x_copy(i, c).wait_send()
    o_copy(oh).wait_recv()
    for side in range(2):
        for c in range(CHUNKS):
            part = o_buf[side, c].astype(F32)
            for j in range(2):
                at = side * half + c * ck + j * cq
                out_ref[:, at : at + cq] = part[j * ns : (j + 1) * ns].astype(BF16)
    o_copy(h).wait_send()


def per_device(
    pool,
    tokens, queries, cache_latent, page_lists, cache_lengths, value_up, out_proj, norm_gain,
    expert_ids, route_weights, gate_proj, up_proj, down_proj,
):
    ns, width = tokens.shape
    _, nh, kdim = queries.shape
    ctx = cache_latent.shape[1]
    _, hh_n, latent, vdim = value_up.shape
    hidden = gate_proj.shape[2]
    half = width // 2
    ck = half // CHUNKS
    cq = ck // 2
    toks = pool * ns
    dma = pltpu.SemaphoreType.DMA
    anywhere = pl.BlockSpec(memory_space=pl.ANY)
    vmem = pl.BlockSpec(memory_space=pltpu.VMEM)
    return pl.pallas_call(
        functools.partial(kernel, pool),
        out_shape=jax.ShapeDtypeStruct((ns, width), BF16),
        in_specs=[
            anywhere, anywhere, anywhere, vmem, vmem, anywhere, anywhere, vmem, vmem, vmem,
            anywhere, anywhere, anywhere,
        ],
        out_specs=vmem,
        scratch_shapes=[
            pltpu.VMEM((ns, width), BF16),
            pltpu.VMEM((ns, nh, kdim), BF16),
            pltpu.VMEM((ns, ctx, kdim), BF16),
            pltpu.VMEM((hh_n, latent, vdim), BF16),
            pltpu.VMEM((hh_n * vdim, width), BF16),
            pltpu.VMEM((width, hidden), BF16),
            pltpu.VMEM((width, hidden), BF16),
            pltpu.VMEM((hidden, width), BF16),
            pltpu.VMEM((ns, nh, ctx), F32),
            pltpu.VMEM((ns * nh, latent), BF16),
            pltpu.VMEM((pool, ns * hh_n, latent), BF16),
            pltpu.VMEM((pool, ns * hh_n, latent), BF16),
            pltpu.VMEM((2, CHUNKS, toks, ck), BF16),
            pltpu.VMEM((2, CHUNKS, toks, ck), BF16),
            pltpu.VMEM((2, CHUNKS, pool, 2 * ns, cq), BF16),
            pltpu.VMEM((2, CHUNKS, pool, 2 * ns, cq), BF16),
            pltpu.VMEM((2, pool, 2 * ns, CHUNKS * cq + 128), BF16),
            pltpu.VMEM((CHUNKS, 2 * ns, cq), F32),
            pltpu.VMEM((2, CHUNKS, 2 * ns, cq), BF16),
            dma((ns,)), dma((7,)),
            dma((pool,)), dma((pool,)),
            dma((2, CHUNKS)), dma((2, CHUNKS)),
            dma((2, CHUNKS, pool)), dma((2, CHUNKS, pool)),
            dma((pool,)), dma((pool,)),
            dma((pool,)), dma((pool,)),
            dma((1,)), dma((1,)),
        ],
        compiler_params=pltpu.CompilerParams(
            collective_id=0, has_side_effects=True, vmem_limit_bytes=60 * 1024 * 1024
        ),
        name="decode_layer",
    )(
        tokens, queries, cache_latent, page_lists, cache_lengths.reshape(ns, 1),
        value_up.reshape(hh_n, latent, vdim), out_proj.reshape(hh_n * vdim, width),
        norm_gain.reshape(1, width), expert_ids, route_weights,
        gate_proj.reshape(width, hidden), up_proj.reshape(width, hidden),
        down_proj.reshape(hidden, width),
    )


def solution(mesh):
    return jax.shard_map(
        functools.partial(per_device, mesh.shape["pool"]),
        mesh=mesh,
        in_specs=(
            P(("groups", "pool"), None),
            P(("groups", "pool"), "head", None),
            P(("groups", "pool"), None, None),
            P(("groups", "pool"), None),
            P(("groups", "pool")),
            P("head", "pool", None, None),
            P("head", "pool", None, None),
            P(),
            P(("groups", "pool"), None),
            P(("groups", "pool"), None),
            P("pool", None, "head"),
            P("pool", None, "head"),
            P("pool", "head", None),
        ),
        out_specs=P(("groups", "pool"), None),
        check_vma=False,
    )
```

time: 228 us -> 80 us (0.35)
  waiting for transfers between devices: 97.7 us -> 0 us
  blocking collectives: 71.7 us -> 0 us
  Pallas kernels: 0 us -> 64.3 us
  matrix products: 22.8 us -> 0 us
  between operations: 13.3 us -> 0.01 us
  other arithmetic: 7.48 us -> 0 us
    all_to_all x3 -> x0, blocking collectives: 71.7 us -> none  [the longest x1 29.3 us: per_device(): lax.all_to_all(outgoing, 'pool', split_axis=0, concat_axis=0, tiled=True)]
    pallas_call x0 -> x1, Pallas kernels: none -> 64.3 us  [per_device(): pl.pallas_call(functools.partial(kernel, pool), out_shape=jax.ShapeDtypeS...]
    reduce_scatter x1 -> x0, waiting for transfers between devices: 61.8 us -> none  [per_device(): lax.psum_scatter(jnp.einsum('shv,hvd->sd', head_values, out_proj[0], pref...]
    psum x2 -> x0, waiting for transfers between devices: 35.8 us -> none  [the longest x1 19.2 us: per_device(): attn_out = lax.psum(attn_part, 'head').astype(jnp.float32)]
    dot_general x7 -> x0, matrix products: 22.8 us -> none  [the longest x1 7.91 us: per_device(): jnp.dot(activated, down_proj[0], preferred_element_type=jnp.float32)]
    gather x3 -> x0, local copies, waits for them, and re-layouts: 5.07 us -> none  [attend(): jnp.take_along_axis(pages, page_lists[:, :, None, None], axis=1)]
    unnamed x20 -> x5, local copies, waits for them, and re-layouts: 8.49 us -> 13.3 us
  transfers between devices with their start and end apart: 3 -> 0, of which waited for: 3 -> 0; matrix products, arithmetic and copies ran while one was open for 0% -> 0% of each run, Pallas kernels for 0% -> 0%
where the time goes in v1:
time: 80 us; the launch traced here: 78.9 us
  Pallas kernels  64.3 us (80%)
  local copies, waits for them, and re-layouts  14.6 us (18%)
    pallas_call x1, Pallas kernels, per_device(): pl.pallas_call(functools.partial(kernel, pool), out_shape=jax.ShapeDtypeS...  64.3 us
    unnamed x5, local copies, waits for them, and re-layouts  13.3 us

profile of v1, /device:TPU:0, one launch (start us, length us, event | category | flops | bytes accessed | tf_op | source)
XLA Modules:
  0.0 78.9 jit_solution(15263117946045885074)
XLA Ops:
  0.0 1.3 %copy.15.pages_ref = s32[8,4]{1,0:T(8,128)} copy(s32[8,4]{0,1:T(4,128)} %param.16) | data formatting | bytes 256 | tf_op args[3]
  1.3 1.3 %copy.16.lens_ref = s32[8,1]{1,0:T(8,128)} copy(s32[8,1]{0,1:T(1,128)} %bitcast.13) | data formatting | bytes 64 | tf_op jit(solution)/shard_map/reshape | solution.py:344
  2.7 1.3 %copy.17.ids_ref = s32[8,2]{1,0:T(8,128)} copy(s32[8,2]{0,1:T(2,128)} %param.21) | data formatting | bytes 128 | tf_op args[8]
  4.0 1.3 %copy.18.rw_ref = f32[8,2]{1,0:T(8,128)} copy(f32[8,2]{0,1:T(2,128)} %param.22) | data formatting | bytes 128 | tf_op args[9]
  5.4 7.7 %copy.14.cache_hbm = bf16[8,512,576]{2,1,0:T(8,128)(2,1)} copy(bf16[8,512,576]{1,2,0:T(8,128)(2,1)} %param.15) | data formatting | bytes 9437184 | tf_op args[2]
  13.0 64.3 %decode_layer.1 = bf16[8,7168]{1,0:T(8,128)(2,1)} custom-call(bf16[8,7168]{1,0:T(8,128)(2,1)} %tok_hbm.1, bf16[8,32,576]{2,1,0:T(8,128)(2,1)} %q_hbm.1, bf16[8,512,576]{2,1,0:T(8,128)(2,1)} %copy.14.cache_hbm, s32[8,4]{1,0:T(8,128)} %copy.15.pages_ref, s32[8,1]{1,0:T(8,128)} %copy.16.lens_ref, bf16[4,512,128]{2,1,0:T(8,128)(2,1)} %bitcast.11, ...), custom_call_target="tpu_custom_call" | custom-call | tf_op jit(solution)/shard_map/decode_layer/pallas_call | solution.py:303
  77.3 1.6 %copy.20 = bf16[8,7168]{1,0:T(8,128)(2,1)} copy(bf16[8,7168]{1,0:T(8,128)(2,1)} %decode_layer.1) | data formatting | bytes 229376

commit v2 on v1

--- a/solution.py
+++ b/solution.py
@@ -39,7 +39,7 @@
     h = lax.axis_index("head")
     oh = 1 - h
     ns, nh, _ = q.shape
-    ctx = cache.shape[1]
+    ctx = cache.shape[2]
     hh_n = vu.shape[0]
     width = tok.shape[1]
     half = width // 2
@@ -99,23 +99,31 @@
 
     pos = lax.broadcasted_iota(jnp.int32, (ns, ctx), 1)
     page = pos >> log2(PAGE)
-    listed = pages_ref[:, 0:1] == page
-    for j in range(1, pages_ref.shape[1]):
-        listed = listed | (pages_ref[:, j : j + 1] == page)
-    usable = jnp.where(listed & (pos < lens_ref[:, 0:1]), 1.0, 0.0)
+    eye = lax.broadcasted_iota(jnp.int32, (ns, ns), 0) == lax.broadcasted_iota(jnp.int32, (ns, ns), 1)
+
+    def column(row):
+        return jnp.sum(jnp.where(eye, row, 0.0), axis=-1, keepdims=True)
+
+    def whole(row):
+        return column(row.astype(F32)).astype(jnp.int32)
+
+    listed = whole(pages_ref[0:1, :]) == page
+    for j in range(1, pages_ref.shape[0]):
+        listed = listed | (whole(pages_ref[j : j + 1, :]) == page)
+    usable = jnp.where(listed & (pos < whole(lens_ref[0:1, :])), 1.0, 0.0)
     load_q.wait()
     for s in range(ns):
         load_k[s].wait()
-        scores[s] = lax.dot_general(
-            q[s], cache[s], (((1,), (1,)), ((), ())), preferred_element_type=F32
-        )
+        scores[s] = dot(q[s], cache[s])
     for s in range(ns):
         keep = usable[s : s + 1, :] > 0.5
         sc = jnp.where(keep, scores[s] * SCALE, -1e30)
         top = jnp.max(sc, axis=-1, keepdims=True)
         weighed = jnp.where(keep, jnp.exp(sc - top), 0.0)
         probs = (weighed / jnp.sum(weighed, axis=-1, keepdims=True)).astype(BF16)
-        lat[s * nh : (s + 1) * nh, :] = dot(probs, cache[s, :, :LATENT]).astype(BF16)
+        lat[s * nh : (s + 1) * nh, :] = lax.dot_general(
+            probs, cache[s, :LATENT, :], (((1,), (1,)), ((), ())), preferred_element_type=F32
+        ).astype(BF16)
 
     per = ns * hh_n
     ri = lax.broadcasted_iota(jnp.int32, (rows, 1), 0)
@@ -201,8 +209,9 @@
     lane = lax.broadcasted_iota(jnp.int32, (ns, 128), 1)
     extra = jnp.broadcast_to(squares, (ns, 128))
     extra = jnp.where(lane < EXPERTS, 0.0, extra)
-    for k in range(ids_ref.shape[1]):
-        extra = extra + jnp.where(lane == ids_ref[:, k : k + 1], rw_ref[:, k : k + 1], 0.0)
+    for k in range(ids_ref.shape[0]):
+        routed = lane == whole(ids_ref[k : k + 1, :])
+        extra = extra + jnp.where(routed, column(rw_ref[k : k + 1, :]), 0.0)
     upper = extra.astype(BF16).astype(F32)
     c_recv[h, p, :, block_w:] = jnp.concatenate([upper, extra - upper], axis=0).astype(BF16)
 
@@ -311,7 +320,7 @@
         scratch_shapes=[
             pltpu.VMEM((ns, width), BF16),
             pltpu.VMEM((ns, nh, kdim), BF16),
-            pltpu.VMEM((ns, ctx, kdim), BF16),
+            pltpu.VMEM((ns, kdim, ctx), BF16),
             pltpu.VMEM((hh_n, latent, vdim), BF16),
             pltpu.VMEM((hh_n * vdim, width), BF16),
             pltpu.VMEM((width, hidden), BF16),
@@ -341,9 +350,9 @@
         ),
         name="decode_layer",
     )(
-        tokens, queries, cache_latent, page_lists, cache_lengths.reshape(ns, 1),
+        tokens, queries, jnp.swapaxes(cache_latent, 1, 2), page_lists.T, cache_lengths.reshape(1, ns),
         value_up.reshape(hh_n, latent, vdim), out_proj.reshape(hh_n * vdim, width),
-        norm_gain.reshape(1, width), expert_ids, route_weights,
+        norm_gain.reshape(1, width), expert_ids.T, route_weights.T,
         gate_proj.reshape(width, hidden), up_proj.reshape(width, hidden),
         down_proj.reshape(hidden, width),
     )

time: 80 us -> 67.2 us (0.84)
  local copies, waits for them, and re-layouts: 14.6 us -> 1.55 us
    unnamed x5 -> x1, local copies, waits for them, and re-layouts: 13.3 us -> 1.55 us
    reshape x1 -> x0, local copies, waits for them, and re-layouts: 1.32 us -> none  [per_device(): cache_lengths.reshape(ns, 1)]
where the time goes in v2:
time: 67.2 us; the launch traced here: 66.3 us
  Pallas kernels  64.8 us (96%)
  local copies, waits for them, and re-layouts  1.55 us (2%)
    pallas_call x1, Pallas kernels, per_device(): pl.pallas_call(functools.partial(kernel, pool), out_shape=jax.ShapeDtypeS...  64.8 us
    unnamed x1, local copies, waits for them, and re-layouts  1.55 us

profile of v2, /device:TPU:0, one launch (start us, length us, event | category | flops | bytes accessed | tf_op | source)
XLA Modules:
  0.0 66.3 jit_solution(15123929229089613844)
XLA Ops:
  0.0 64.8 %decode_layer.1 = bf16[8,7168]{1,0:T(8,128)(2,1)} custom-call(bf16[8,7168]{1,0:T(8,128)(2,1)} %tok_hbm.1, bf16[8,32,576]{2,1,0:T(8,128)(2,1)} %q_hbm.1, bf16[8,576,512]{2,1,0:T(8,128)(2,1)} %bitcast.15, s32[4,8]{1,0:T(4,128)} %bitcast.18, s32[1,8]{1,0:T(1,128)} %bitcast.21, bf16[4,512,128]{2,1,0:T(8,128)(2,1)} %bitcast.16, bf16[512,7168]{1,0:T(8,128)(2,1)} %bitcast.11, ...), custom_call_target="tpu_custom_call" | custom-call | tf_op jit(solution)/shard_map/decode_layer/pallas_call | solution.py:312
  64.8 1.6 %copy.15 = bf16[8,7168]{1,0:T(8,128)(2,1)} copy(bf16[8,7168]{1,0:T(8,128)(2,1)} %decode_layer.1) | data formatting | bytes 229376

commit v3 on v2

--- a/solution.py
+++ b/solution.py
@@ -10,7 +10,7 @@
 LATENT = 512
 EXPERTS = 4
 PAGE = 64
-CHUNKS = 2
+CHUNKS = 7
 SCALE = 192 ** (-0.5)
 MESH = pl.DeviceIdType.MESH
 BF16 = jnp.bfloat16
@@ -32,12 +32,17 @@
     g_hbm, u_hbm, d_hbm,
     out_ref,
     tok, q, cache, vu, op, gw, uw, dw,
-    scores, lat, a_buf, a_recv, x_buf, x_recv, r_buf, r_recv, c_recv, resid, o_buf,
-    k_sem, w_sem, a_s, a_r, x_s, x_r, r_s, r_r, c_s, c_r, f_s, f_r, o_s, o_r,
+    scores, lat, a_buf, a_recv, x_buf, x_recv, y_buf, y_recv, r_buf, r_recv, c_recv, resid, o_buf,
+    k_sem, w_sem, a_s, a_r, x_s, x_r, y_s, y_r, r_s, r_r, c_s, c_r,
+    g_s, g_r, f_s, f_r, o_s, o_r,
 ):
     p = lax.axis_index("pool")
     h = lax.axis_index("head")
     oh = 1 - h
+    lines = pool // 2
+    z = p // 2
+    y = lax.rem(p, 2)
+    beside = z * 2 + 1 - y
     ns, nh, _ = q.shape
     ctx = cache.shape[2]
     hh_n = vu.shape[0]
@@ -60,7 +65,7 @@
     load_g = pltpu.make_async_copy(g_hbm, gw, w_sem.at[4])
     load_u = pltpu.make_async_copy(u_hbm, uw, w_sem.at[5])
     load_d = pltpu.make_async_copy(d_hbm, dw, w_sem.at[6])
-    for copy in (load_vu, load_op, load_tok, load_g, load_u, load_d):
+    for copy in (load_vu, load_op, load_tok):
         copy.start()
 
     def peer(d):
@@ -90,12 +95,18 @@
             device_id={"head": oh}, device_id_type=MESH,
         )
 
-    def each(body):
+    def each(body, low=1, high=pool):
         def step(d, carry):
             body(d)
             return carry
 
-        lax.fori_loop(1, pool, step, 0)
+        lax.fori_loop(low, high, step, 0)
+
+    def ahead(d):
+        return lax.rem(z + d, lines)
+
+    def behind(d):
+        return lax.rem(z + lines - d, lines)
 
     pos = lax.broadcasted_iota(jnp.int32, (ns, ctx), 1)
     page = pos >> log2(PAGE)
@@ -112,42 +123,55 @@
         listed = listed | (whole(pages_ref[j : j + 1, :]) == page)
     usable = jnp.where(listed & (pos < whole(lens_ref[0:1, :])), 1.0, 0.0)
     load_q.wait()
-    for s in range(ns):
-        load_k[s].wait()
-        scores[s] = dot(q[s], cache[s])
-    for s in range(ns):
-        keep = usable[s : s + 1, :] > 0.5
-        sc = jnp.where(keep, scores[s] * SCALE, -1e30)
-        top = jnp.max(sc, axis=-1, keepdims=True)
-        weighed = jnp.where(keep, jnp.exp(sc - top), 0.0)
-        probs = (weighed / jnp.sum(weighed, axis=-1, keepdims=True)).astype(BF16)
-        lat[s * nh : (s + 1) * nh, :] = lax.dot_general(
-            probs, cache[s, :LATENT, :], (((1,), (1,)), ((), ())), preferred_element_type=F32
-        ).astype(BF16)
-
-    per = ns * hh_n
-    ri = lax.broadcasted_iota(jnp.int32, (rows, 1), 0)
+    groups = a_buf.shape[0]
+    gs = ns // groups
+    per = gs * hh_n
+    some = gs * nh
+    ri = lax.broadcasted_iota(jnp.int32, (some, 1), 0)
     rest = ri & (per - 1)
     origin = (rest >> log2(hh_n)) * nh + (ri >> log2(per)) * hh_n + (rest & (hh_n - 1))
-    ci = lax.broadcasted_iota(jnp.int32, (rows, rows), 1)
+    ci = lax.broadcasted_iota(jnp.int32, (some, some), 1)
     perm = jnp.where(ci == origin, 1.0, 0.0).astype(BF16)
-    a_buf[...] = dot(perm, lat[...]).reshape(pool, per, LATENT).astype(BF16)
-    pl.semaphore_wait(barrier, pool)
-
-    def a_copy(d, slot):
-        return to_pool(a_buf.at[peer(d)], a_recv.at[slot], a_s.at[d], a_r.at[d], peer(d))
-
-    each(lambda d: a_copy(d, p).start())
-    a_recv[p] = a_buf[p]
+
+    def a_copy(g, d, slot):
+        return to_pool(a_buf.at[g, peer(d)], a_recv.at[g, slot], a_s.at[g, d], a_r.at[g, d], peer(d))
+
+    for g in range(groups):
+        streams = range(g * gs, (g + 1) * gs)
+        for s in streams:
+            load_k[s].wait()
+            scores[s] = dot(q[s], cache[s])
+        if g == groups - 1:
+            for copy in (load_g, load_u, load_d):
+                copy.start()
+        for s in streams:
+            keep = usable[s : s + 1, :] > 0.5
+            sc = jnp.where(keep, scores[s] * SCALE, -1e30)
+            top = jnp.max(sc, axis=-1, keepdims=True)
+            weighed = jnp.where(keep, jnp.exp(sc - top), 0.0)
+            probs = (weighed / jnp.sum(weighed, axis=-1, keepdims=True)).astype(BF16)
+            lat[s * nh : (s + 1) * nh, :] = lax.dot_general(
+                probs, cache[s, :LATENT, :], (((1,), (1,)), ((), ())), preferred_element_type=F32
+            ).astype(BF16)
+        sent_rows = dot(perm, lat[g * some : (g + 1) * some, :])
+        a_buf[g] = sent_rows.reshape(pool, per, LATENT).astype(BF16)
+        if g == 0:
+            pl.semaphore_wait(barrier, pool)
+        each(lambda d: a_copy(g, d, p).start())
+        a_recv[g, p] = a_buf[g, p]
     load_vu.wait()
-    each(lambda d: a_copy(d, source(d)).wait_recv())
+    for g in range(groups):
+        each(lambda d: a_copy(g, d, source(d)).wait_recv())
     got = a_recv[...].astype(F32).reshape(rows, LATENT).astype(BF16)
     values = []
-    ti = lax.broadcasted_iota(jnp.int32, (toks, rows), 0)
+    ti = lax.broadcasted_iota(jnp.int32, (toks, 1), 0)
     tj = lax.broadcasted_iota(jnp.int32, (toks, rows), 1)
     for hh in range(hh_n):
         if hh_n > 1:
-            pick = jnp.where(tj == ti * hh_n + hh, 1.0, 0.0).astype(BF16)
+            inside = ti & (ns - 1)
+            spot = (inside >> log2(gs)) * pool + (ti >> log2(ns))
+            spot = (spot * gs + (inside & (gs - 1))) * hh_n + hh
+            pick = jnp.where(tj == spot, 1.0, 0.0).astype(BF16)
             mine = dot(pick, got).astype(BF16)
         else:
             mine = got
@@ -157,9 +181,13 @@
     def x_copy(i, c):
         return to_core(x_buf.at[i, c], x_recv.at[i, c], x_s.at[i, c], x_r.at[i, c])
 
+    def y_copy(i, c):
+        return to_pool(y_buf.at[i, c, 1 - y], y_recv.at[i, c], y_s.at[i, c], y_r.at[i, c], beside)
+
     def r_copy(i, c, d, slot):
         return to_pool(
-            r_buf.at[i, c, peer(d)], r_recv.at[i, c, slot], r_s.at[i, c, d], r_r.at[i, c, d], peer(d)
+            r_buf.at[i, c, ahead(d)], r_recv.at[i, c, slot], r_s.at[i, c, d], r_r.at[i, c, d],
+            ahead(d) * 2 + y,
         )
 
     def columns(side, c, j=0, size=ck):
@@ -178,14 +206,19 @@
                 v = v * by
             x_copy(i, c).wait_recv()
             v = v + x_recv[i, c].astype(F32)
-            low = v[:, :cq].reshape(pool, ns, cq)
-            high = v[:, cq:].reshape(pool, ns, cq)
-            r_buf[i, c] = jnp.concatenate([low, high], axis=1).astype(BF16)
-            each(lambda d: r_copy(i, c, d, p).start())
-            r_recv[i, c, p] = r_buf[i, c, p]
+            low = v[:, :cq].reshape(lines, 2, ns, cq)
+            high = v[:, cq:].reshape(lines, 2, ns, cq)
+            for side in range(2):
+                y_buf[i, c, side] = jnp.concatenate([low[:, side], high[:, side]], axis=1).astype(BF16)
+            y_copy(i, c).start()
+        for c in range(CHUNKS):
+            y_copy(i, c).wait_recv()
+            r_buf[i, c] = (y_buf[i, c, y].astype(F32) + y_recv[i, c].astype(F32)).astype(BF16)
+            each(lambda d: r_copy(i, c, d, z).start(), 1, lines)
+            r_recv[i, c, z] = r_buf[i, c, z]
 
     def reduced(i, c):
-        each(lambda d: r_copy(i, c, d, source(d)).wait_recv())
+        each(lambda d: r_copy(i, c, d, behind(d)).wait_recv(), 1, lines)
         return jnp.sum(r_recv[i, c].astype(F32), axis=0)
 
     load_op.wait()
@@ -215,22 +248,36 @@
     upper = extra.astype(BF16).astype(F32)
     c_recv[h, p, :, block_w:] = jnp.concatenate([upper, extra - upper], axis=0).astype(BF16)
 
-    def c_copy(d, slot):
-        return to_pool(c_recv.at[h, slot], c_recv.at[h, slot], c_s.at[d], c_r.at[d], peer(d))
-
-    def f_copy(d, side, slot):
-        return to_core(c_recv.at[side, slot], c_recv.at[side, slot], f_s.at[d], f_r.at[d])
-
-    each(lambda d: c_copy(d, p).start())
-    f_copy(0, h, p).start()
+    def c_copy(d, line):
+        slot = line * 2 + y
+        block = c_recv.at[h, slot]
+        return to_pool(block, block, c_s.at[d], c_r.at[d], ahead(d) * 2 + y)
+
+    def g_copy(d, side):
+        block = c_recv.at[h, behind(d) * 2 + side]
+        return to_pool(block, block, g_s.at[d], g_r.at[d], beside)
+
+    def f_copy(d, far, half_of):
+        slot = behind(d) * 2 + (1 - y if far else y)
+        block = c_recv.at[half_of, slot]
+        return to_core(block, block, f_s.at[far, d], f_r.at[far, d])
+
+    each(lambda d: c_copy(d, z).start(), 1, lines)
+    g_copy(0, y).start()
+    f_copy(0, 0, h).start()
     load_g.wait()
     load_u.wait()
 
     def pass_on(d):
-        c_copy(d, source(d)).wait_recv()
-        f_copy(d, h, source(d)).start()
-
-    each(pass_on)
+        c_copy(d, behind(d)).wait_recv()
+        g_copy(d, y).start()
+        f_copy(d, 0, h).start()
+        g_copy(d - 1, 1 - y).wait_recv()
+        f_copy(d - 1, 1, h).start()
+
+    each(pass_on, 1, lines)
+    g_copy(lines - 1, 1 - y).wait_recv()
+    f_copy(lines - 1, 1, h).start()
 
     def project(side):
         gate = up = None
@@ -247,8 +294,8 @@
         return gate, up, (part[:, :ns] + part[:, ns:]).reshape(toks, 128)
 
     gate0, up0, extra0 = project(h)
-    f_copy(0, oh, p).wait_recv()
-    each(lambda d: f_copy(d, oh, source(d)).wait_recv())
+    for far in range(2):
+        each(lambda d: f_copy(d, far, oh).wait_recv(), 0, lines)
     gate1, up1, extra1 = project(oh)
     lane = lax.broadcasted_iota(jnp.int32, (toks, 128), 1)
     expert = p // (pool // EXPERTS)
@@ -270,18 +317,27 @@
     o_copy(h).start()
 
     def sent(d):
-        a_copy(d, p).wait_send()
-        c_copy(d, p).wait_send()
-        f_copy(d, h, source(d)).wait_send()
+        for g in range(groups):
+            a_copy(g, d, p).wait_send()
+
+    def sent_line(d):
+        c_copy(d, z).wait_send()
         for i in range(2):
             for c in range(CHUNKS):
-                r_copy(i, c, d, p).wait_send()
+                r_copy(i, c, d, z).wait_send()
+
+    def sent_near(d):
+        g_copy(d, y).wait_send()
+        for far in range(2):
+            f_copy(d, far, h).wait_send()
 
     each(sent)
-    f_copy(0, h, p).wait_send()
+    each(sent_line, 1, lines)
+    each(sent_near, 0, lines)
     for i in range(2):
         for c in range(CHUNKS):
             x_copy(i, c).wait_send()
+            y_copy(i, c).wait_send()
     o_copy(oh).wait_recv()
     for side in range(2):
         for c in range(CHUNKS):
@@ -306,6 +362,8 @@
     ck = half // CHUNKS
     cq = ck // 2
     toks = pool * ns
+    lines = pool // 2
+    groups = 2 if ns * hh_n >= 32 else 1
     dma = pltpu.SemaphoreType.DMA
     anywhere = pl.BlockSpec(memory_space=pl.ANY)
     vmem = pl.BlockSpec(memory_space=pltpu.VMEM)
@@ -328,21 +386,25 @@
             pltpu.VMEM((hidden, width), BF16),
             pltpu.VMEM((ns, nh, ctx), F32),
             pltpu.VMEM((ns * nh, latent), BF16),
-            pltpu.VMEM((pool, ns * hh_n, latent), BF16),
-            pltpu.VMEM((pool, ns * hh_n, latent), BF16),
+            pltpu.VMEM((groups, pool, ns // groups * hh_n, latent), BF16),
+            pltpu.VMEM((groups, pool, ns // groups * hh_n, latent), BF16),
             pltpu.VMEM((2, CHUNKS, toks, ck), BF16),
             pltpu.VMEM((2, CHUNKS, toks, ck), BF16),
-            pltpu.VMEM((2, CHUNKS, pool, 2 * ns, cq), BF16),
-            pltpu.VMEM((2, CHUNKS, pool, 2 * ns, cq), BF16),
+            pltpu.VMEM((2, CHUNKS, 2, lines, 2 * ns, cq), BF16),
+            pltpu.VMEM((2, CHUNKS, lines, 2 * ns, cq), BF16),
+            pltpu.VMEM((2, CHUNKS, lines, 2 * ns, cq), BF16),
+            pltpu.VMEM((2, CHUNKS, lines, 2 * ns, cq), BF16),
             pltpu.VMEM((2, pool, 2 * ns, CHUNKS * cq + 128), BF16),
             pltpu.VMEM((CHUNKS, 2 * ns, cq), F32),
             pltpu.VMEM((2, CHUNKS, 2 * ns, cq), BF16),
             dma((ns,)), dma((7,)),
-            dma((pool,)), dma((pool,)),
+            dma((groups, pool)), dma((groups, pool)),
             dma((2, CHUNKS)), dma((2, CHUNKS)),
-            dma((2, CHUNKS, pool)), dma((2, CHUNKS, pool)),
-            dma((pool,)), dma((pool,)),
-            dma((pool,)), dma((pool,)),
+            dma((2, CHUNKS)), dma((2, CHUNKS)),
+            dma((2, CHUNKS, lines)), dma((2, CHUNKS, lines)),
+            dma((lines,)), dma((lines,)),
+            dma((lines,)), dma((lines,)),
+            dma((2, lines)), dma((2, lines)),
             dma((1,)), dma((1,)),
         ],
         compiler_params=pltpu.CompilerParams(

time: 67.2 us -> 57.7 us (0.86); the launches traced: 66.3 us -> 57.5 us
  Pallas kernels: 64.8 us -> 56 us
    pallas_call x1, Pallas kernels: 64.8 us -> 56 us  [per_device(): pl.pallas_call(functools.partial(kernel, pool), out_shape=jax.ShapeDtypeS...]
where the time goes in v3:
time: 57.7 us; the launch traced here: 57.5 us
  Pallas kernels  56 us (97%)
  local copies, waits for them, and re-layouts  1.55 us (3%)
    pallas_call x1, Pallas kernels, per_device(): pl.pallas_call(functools.partial(kernel, pool), out_shape=jax.ShapeDtypeS...  56 us
    unnamed x1, local copies, waits for them, and re-layouts  1.55 us

profile of v3, /device:TPU:0, one launch (start us, length us, event | category | flops | bytes accessed | tf_op | source)
XLA Modules:
  0.0 57.5 jit_solution(2304953243374700350)
XLA Ops:
  0.0 56.0 %decode_layer.1 = bf16[8,7168]{1,0:T(8,128)(2,1)} custom-call(bf16[8,7168]{1,0:T(8,128)(2,1)} %tok_hbm.1, bf16[8,32,576]{2,1,0:T(8,128)(2,1)} %q_hbm.1, bf16[8,576,512]{2,1,0:T(8,128)(2,1)} %bitcast.15, s32[4,8]{1,0:T(4,128)} %bitcast.18, s32[1,8]{1,0:T(1,128)} %bitcast.21, bf16[4,512,128]{2,1,0:T(8,128)(2,1)} %bitcast.16, bf16[512,7168]{1,0:T(8,128)(2,1)} %bitcast.11, ...), custom_call_target="tpu_custom_call" | custom-call | tf_op jit(solution)/shard_map/decode_layer/pallas_call | solution.py:370
  56.0 1.6 %copy.15 = bf16[8,7168]{1,0:T(8,128)(2,1)} copy(bf16[8,7168]{1,0:T(8,128)(2,1)} %decode_layer.1) | data formatting | bytes 229376

commit v4 on v3

--- a/solution.py
+++ b/solution.py
@@ -11,6 +11,7 @@
 EXPERTS = 4
 PAGE = 64
 CHUNKS = 7
+PARTS = 2
 SCALE = 192 ** (-0.5)
 MESH = pl.DeviceIdType.MESH
 BF16 = jnp.bfloat16
@@ -248,36 +249,49 @@
     upper = extra.astype(BF16).astype(F32)
     c_recv[h, p, :, block_w:] = jnp.concatenate([upper, extra - upper], axis=0).astype(BF16)
 
-    def c_copy(d, line):
-        slot = line * 2 + y
-        block = c_recv.at[h, slot]
-        return to_pool(block, block, c_s.at[d], c_r.at[d], ahead(d) * 2 + y)
-
-    def g_copy(d, side):
-        block = c_recv.at[h, behind(d) * 2 + side]
-        return to_pool(block, block, g_s.at[d], g_r.at[d], beside)
-
-    def f_copy(d, far, half_of):
-        slot = behind(d) * 2 + (1 - y if far else y)
-        block = c_recv.at[half_of, slot]
-        return to_core(block, block, f_s.at[far, d], f_r.at[far, d])
-
-    each(lambda d: c_copy(d, z).start(), 1, lines)
-    g_copy(0, y).start()
-    f_copy(0, 0, h).start()
+    lanes = -(-(block_w + 128) // (PARTS * 128)) * 128
+    spans = [pl.ds(k * lanes, min(lanes, block_w + 128 - k * lanes)) for k in range(PARTS)]
+
+    def c_copy(k, d, line):
+        block = c_recv.at[h, line * 2 + y, :, spans[k]]
+        return to_pool(block, block, c_s.at[k, d], c_r.at[k, d], ahead(d) * 2 + y)
+
+    def g_copy(k, d, side):
+        block = c_recv.at[h, behind(d) * 2 + side, :, spans[k]]
+        return to_pool(block, block, g_s.at[k, d], g_r.at[k, d], beside)
+
+    def f_copy(k, d, far, half_of):
+        block = c_recv.at[half_of, behind(d) * 2 + (1 - y if far else y), :, spans[k]]
+        return to_core(block, block, f_s.at[k, far, d], f_r.at[k, far, d])
+
+    for k in range(PARTS):
+        each(lambda d: c_copy(k, d, z).start(), 1, lines)
+        g_copy(k, 0, y).start()
+        f_copy(k, 0, 0, h).start()
     load_g.wait()
     load_u.wait()
-
-    def pass_on(d):
-        c_copy(d, behind(d)).wait_recv()
-        g_copy(d, y).start()
-        f_copy(d, 0, h).start()
-        g_copy(d - 1, 1 - y).wait_recv()
-        f_copy(d - 1, 1, h).start()
-
-    each(pass_on, 1, lines)
-    g_copy(lines - 1, 1 - y).wait_recv()
-    f_copy(lines - 1, 1, h).start()
+    for k in range(PARTS):
+
+        def pass_on(d):
+            c_copy(k, d, behind(d)).wait_recv()
+            g_copy(k, d, y).start()
+            f_copy(k, d, 0, h).start()
+
+        def pass_far(d):
+            g_copy(k, d, 1 - y).wait_recv()
+            f_copy(k, d, 1, h).start()
+
+        each(pass_on, 1, lines)
+        if k > 0:
+            last = k - 1
+
+            def pass_last(d):
+                g_copy(last, d, 1 - y).wait_recv()
+                f_copy(last, d, 1, h).start()
+
+            each(pass_last, 0, lines)
+        if k == PARTS - 1:
+            each(pass_far, 0, lines)
 
     def project(side):
         gate = up = None
@@ -294,8 +308,9 @@
         return gate, up, (part[:, :ns] + part[:, ns:]).reshape(toks, 128)
 
     gate0, up0, extra0 = project(h)
-    for far in range(2):
-        each(lambda d: f_copy(d, far, oh).wait_recv(), 0, lines)
+    for k in range(PARTS):
+        for far in range(2):
+            each(lambda d: f_copy(k, d, far, oh).wait_recv(), 0, lines)
     gate1, up1, extra1 = project(oh)
     lane = lax.broadcasted_iota(jnp.int32, (toks, 128), 1)
     expert = p // (pool // EXPERTS)
@@ -321,15 +336,17 @@
             a_copy(g, d, p).wait_send()
 
     def sent_line(d):
-        c_copy(d, z).wait_send()
+        for k in range(PARTS):
+            c_copy(k, d, z).wait_send()
         for i in range(2):
             for c in range(CHUNKS):
                 r_copy(i, c, d, z).wait_send()
 
     def sent_near(d):
-        g_copy(d, y).wait_send()
-        for far in range(2):
-            f_copy(d, far, h).wait_send()
+        for k in range(PARTS):
+            g_copy(k, d, y).wait_send()
+            for far in range(2):
+                f_copy(k, d, far, h).wait_send()
 
     each(sent)
     each(sent_line, 1, lines)
@@ -402,9 +419,9 @@
             dma((2, CHUNKS)), dma((2, CHUNKS)),
             dma((2, CHUNKS)), dma((2, CHUNKS)),
             dma((2, CHUNKS, lines)), dma((2, CHUNKS, lines)),
-            dma((lines,)), dma((lines,)),
-            dma((lines,)), dma((lines,)),
-            dma((2, lines)), dma((2, lines)),
+            dma((PARTS, lines)), dma((PARTS, lines)),
+            dma((PARTS, lines)), dma((PARTS, lines)),
+            dma((PARTS, 2, lines)), dma((PARTS, 2, lines)),
             dma((1,)), dma((1,)),
         ],
         compiler_params=pltpu.CompilerParams(

time: 57.7 us -> 57.1 us (0.990)
  Pallas kernels: 56 us -> 55.4 us
    pallas_call x1, Pallas kernels: 56 us -> 55.4 us  [per_device(): pl.pallas_call(functools.partial(kernel, pool), out_shape=jax.ShapeDtypeS...]
where the time goes in v4:
time: 57.1 us; the launch traced here: 56.9 us
  Pallas kernels  55.4 us (97%)
  local copies, waits for them, and re-layouts  1.55 us (3%)
    pallas_call x1, Pallas kernels, per_device(): pl.pallas_call(functools.partial(kernel, pool), out_shape=jax.ShapeDtypeS...  55.4 us
    unnamed x1, local copies, waits for them, and re-layouts  1.55 us

profile of v4, /device:TPU:0, one launch (start us, length us, event | category | flops | bytes accessed | tf_op | source)
XLA Modules:
  0.0 56.9 jit_solution(15508812227529632267)
XLA Ops:
  0.0 55.4 %decode_layer.1 = bf16[8,7168]{1,0:T(8,128)(2,1)} custom-call(bf16[8,7168]{1,0:T(8,128)(2,1)} %tok_hbm.1, bf16[8,32,576]{2,1,0:T(8,128)(2,1)} %q_hbm.1, bf16[8,576,512]{2,1,0:T(8,128)(2,1)} %bitcast.15, s32[4,8]{1,0:T(4,128)} %bitcast.18, s32[1,8]{1,0:T(1,128)} %bitcast.21, bf16[4,512,128]{2,1,0:T(8,128)(2,1)} %bitcast.16, bf16[512,7168]{1,0:T(8,128)(2,1)} %bitcast.11, ...), custom_call_target="tpu_custom_call" | custom-call | tf_op jit(solution)/shard_map/decode_layer/pallas_call | solution.py:387
  55.4 1.6 %copy.15 = bf16[8,7168]{1,0:T(8,128)(2,1)} copy(bf16[8,7168]{1,0:T(8,128)(2,1)} %decode_layer.1) | data formatting | bytes 229376
